TPU v7x, 512 devices: a whole 4x8x8 slice. The times are simulated.
512 devices in a mesh: row: 8 (over z), col: 16 (over y, core), layer: 4 (over x).
Axes of the slice: x: 4, y: 8, z: 8, core: 2. Of those that a mesh axis runs over, the one named last changes fastest.
Arguments:
- panel_values: bfloat16 [16384, 8192], P('row', ('layer', 'col')), may hold values from -6 to 6
- slab_values: bfloat16 [8192, 6144], P(('layer', 'row'), 'col'), may hold values from -0.09375 to 0.09375
- pattern_panel: int32 [128, 64], P('row', ('layer', 'col')), may hold values from 0 to 1, as said below
- pattern_result: int32 [128, 48], P(('row', 'layer'), 'col'), may hold values 0 or 1
Outputs:
- product_slab: bfloat16 [16384, 6144], P(('row', 'layer'), 'col')
Inputs may be any that keep to these rules, and one draw needn't show every extreme that they name: `pattern_panel`: in every group of 16 blocks that one device holds of one block column (block rows r * 16 to r * 16 + 15), 1 to 8 are 1; some group reaches this bound: every group of block column 0 has exactly 8.
All inputs are finite; a program needn't handle non-finite values. No bound on the sum of `pattern_result` on one device may be relied on, other than what follows from the above.
Results may differ from a plain program's by a relative error of at most 0.001.
Values may be sent and summed in bfloat16 or wider, within the bound.
A program may use at most 64 MiB of HBM per device.

v0:
```python
import jax
import jax.numpy as jnp
from jax import lax
from jax.sharding import PartitionSpec as P


def per_device(panel_values, slab_values, pattern_panel, pattern_result):
    block = panel_values.shape[1]
    row_blocks = pattern_panel.shape[0]
    gathered = lax.all_gather(slab_values, "row", axis=0, tiled=True)
    flags = pattern_panel[:, 0]
    blocks_here = panel_values.reshape(row_blocks, block, block)
    masked = (blocks_here * flags.astype(jnp.bfloat16)[:, None, None]).reshape(
        row_blocks * block, block
    )
    partial_value = jnp.dot(
        lax.all_gather(masked, "col", axis=1, tiled=True),
        gathered,
        preferred_element_type=jnp.float32,
    )
    shares = lax.psum_scatter(partial_value, "layer", scatter_dimension=0, tiled=True)
    out_blocks = pattern_result.shape[0]
    col_blocks = pattern_result.shape[1]
    keeper = pattern_result.astype(jnp.float32)
    filtered = shares.reshape(out_blocks, block, col_blocks, block) * keeper[:, None, :, None]
    return filtered.reshape(shares.shape).astype(jnp.bfloat16)


def solution(mesh):
    placed = (
        P("row", ("layer", "col")),
        P(("layer", "row"), "col"),
        P("row", ("layer", "col")),
        P(("row", "layer"), "col"),
    )
    return jax.shard_map(
        per_device,
        mesh=mesh,
        in_specs=placed,
        out_specs=P(("row", "layer"), "col"),
        check_vma=False,
    )
```

profile of v0, /device:TPU:1, one launch (start us, length us, event | category | flops | bytes accessed | tf_op | source)
XLA Modules:
  0.0 186.3 jit_solution(16902584694863488766)
XLA Ops:
  6.5 0.0 all-gather.5.cloned.1.call-start
  6.5 0.7 all-gather.5.cloned.1.call-update
  7.3 0.0 all-gather.3.cloned.1.call-start
  7.3 0.7 convert_bitcast_fusion
  8.0 0.1 broadcast_bitcast_fusion
  8.0 2.2 %broadcast_multiply_fusion = bf16[2048,128]{1,0:T(8,128)(2,1)} fusion(bf16[2048,128]{1,0:T(8,128)(2,1)} %param.4, bf16[2048]{0:T(1024)(128)(2,1)S(1)} %broadcast_bitcast_fusion), kind=kLoop, calls=%fused_computation.2 | loop fusion | flops 262144 | bytes 1052672 | tf_op jit(solution)/shard_map/mul | solution.py:13
  10.3 0.0 all-gather.3.cloned.1.call-update
  10.3 0.0 reduce-scatter.2.cloned.1.call-start
  10.3 44.2 %all-gather.5.cloned.1.call-done = bf16[2048,384]{1,0:T(8,128)(2,1)} async-done(((bf16[256,384]{1,0:T(8,128)(2,1)}), bf16[2048,384]{1,0:T(8,128)(2,1)}) %all-gather.5.cloned.1.call-update) | async-done | bytes 1572880 | tf_op jit(solution)/shard_map/all_gather | solution.py:10
  54.5 73.2 %all-gather.3.cloned.1.call-done = bf16[2048,2048]{1,0:T(8,128)(2,1)} async-done(((bf16[2048,128]{1,0:T(8,128)(2,1)}), bf16[2048,2048]{1,0:T(8,128)(2,1)}) %all-gather.3.cloned.1.call-update) | async-done | bytes 8388624 | tf_op jit(solution)/shard_map/all_gather | solution.py:17
  127.7 10.1 %fusion = f32[2048,384]{1,0:T(8,128)} fusion(bf16[2048,2048]{1,0:T(8,128)(2,1)} %all-gather.3.cloned.1.call-done, bf16[2048,384]{1,0:T(8,128)(2,1)} %all-gather.5.cloned.1.call-done), kind=kOutput, calls=%fused_computation.5 | convolution fusion | flops 3221225472 | bytes 13107200 | tf_op jit(solution)/shard_map/dot_general | solution.py:16
  137.8 0.0 copy-start
  137.8 0.0 reduce-scatter.2.cloned.1.call-update
  137.8 0.7 copy-done
  138.4 0.1 copy.5
  138.5 0.2 mul.28
  138.7 0.1 copy.9
  138.8 0.3 copy.6
  139.1 38.8 %reduce-scatter.2.cloned.1.call-done = f32[512,384]{1,0:T(8,128)} async-done(((f32[2048,384]{1,0:T(8,128)}), f32[512,384]{1,0:T(8,128)}) %reduce-scatter.2.cloned.1.call-update) | async-done | bytes 786448 | tf_op jit(solution)/shard_map/reduce_scatter | solution.py:21
  177.8 2.0 %multiply_convert_fusion = bf16[512,384]{1,0:T(8,128)(2,1)} fusion(f32[512,384]{1,0:T(8,128)} %reduce-scatter.2.cloned.1.call-done, f32[512,384]{1,0:T(8,128)S(1)} %copy.6), kind=kLoop, calls=%fused_computation.1 | loop fusion | flops 393216 | bytes 1966080 | tf_op jit(solution)/shard_map/convert_element_type | solution.py:26
  (1 shorter events, 0.0 us)
Async XLA Ops:
  6.5 48.0 %all-gather.5.cloned.1.call-start = ((), (), s32[]{:S(2)}) async-start(), calls=%async_computation.2 | async-start | bytes 1769472 | tf_op jit(solution)/shard_map/all_gather | solution.py:10
  7.3 120.5 %all-gather.3.cloned.1.call-start = ((), (), s32[]{:S(2)}) async-start(), calls=%async_computation.1 | async-start | bytes 8912896 | tf_op jit(solution)/shard_map/all_gather | solution.py:17
  10.3 167.5 %reduce-scatter.2.cloned.1.call-start = ((), (), s32[]{:S(2)}) async-start(), calls=%async_computation.3 | async-start | bytes 3932160 | tf_op jit(solution)/shard_map/reduce_scatter | solution.py:21
  137.8 0.7 copy-start
Sparse Core Ops, SparseCore 0:
  9.4 45.0 all-gather.4
  56.6 71.0 all-gather.2
  137.9 39.8 reduce-scatter.1
where the time goes:
time: 187 us; the launch traced here: 186 us
  waiting for transfers between devices  157 us (84%)
  between operations  13.1 us (7%)
  matrix products  10.1 us (5%)
  other arithmetic  4.83 us (3%)
    all_gather x1, waiting for transfers between devices, per_device(): lax.all_gather(masked, 'col', axis=1, tiled=True)  73.2 us
    all_gather x1, waiting for transfers between devices, per_device(): gathered = lax.all_gather(slab_values, 'row', axis=0, tiled=True)  44.2 us
    reduce_scatter x1, waiting for transfers between devices, per_device(): lax.psum_scatter(partial_value, 'layer', scatter_dimension=0, tiled=True)  38.8 us
    dot_general x1, matrix products, per_device(): jnp.dot(lax.all_gather(masked, 'col', axis=1, tiled=True), gathered, pref...  10.1 us
  transfers between devices with their start and end apart: 3, of which 3 were waited for; matrix products, arithmetic and copies ran while one was open for 2% of the time, Pallas kernels for 0%

commit v1 on v0

--- a/solution.py
+++ b/solution.py
@@ -7,7 +7,12 @@
 def per_device(panel_values, slab_values, pattern_panel, pattern_result):
     block = panel_values.shape[1]
     row_blocks = pattern_panel.shape[0]
-    gathered = lax.all_gather(slab_values, "row", axis=0, tiled=True)
+    ring = [slab_values]
+    for hop in range(7):
+        ring.append(lax.ppermute(ring[-1], "row", [(dev, (dev + 1) % 8) for dev in range(8)]))
+    gathered = jnp.roll(
+        jnp.concatenate(ring[::-1], axis=0), (lax.axis_index("row") + 1) * ring[0].shape[0], axis=0
+    )
     flags = pattern_panel[:, 0]
     blocks_here = panel_values.reshape(row_blocks, block, block)
     masked = (blocks_here * flags.astype(jnp.bfloat16)[:, None, None]).reshape(

time: 187 us -> 152 us (0.81)
  waiting for transfers between devices: 157 us -> 94.3 us
  starting transfers between devices: 0.08 us -> 16.3 us
  local copies, waits for them, and re-layouts: 1.31 us -> 12.5 us
    all_gather x1, waiting for transfers between devices: 73.2 us -> 0.01 us  [per_device(): lax.all_gather(masked, 'col', axis=1, tiled=True)]
    ppermute x0 -> x7, waiting for transfers between devices: none -> 48.1 us  [per_device(): lax.ppermute(ring[-1], 'row', [(dev, (dev + 1) % 8) for dev in range(8)])]
    all_gather x1 -> x0, waiting for transfers between devices: 44.2 us -> none  [per_device(): gathered = lax.all_gather(slab_values, 'row', axis=0, tiled=True)]
    ppermute x0 -> x7, starting transfers between devices: none -> 16.3 us  [per_device(): lax.ppermute(ring[-1], 'row', [(dev, (dev + 1) % 8) for dev in range(8)])]
    unnamed x3 -> x20, local copies, waits for them, and re-layouts: 0.71 us -> 11.2 us
    reduce_scatter x1, waiting for transfers between devices: 38.8 us -> 46.2 us  [per_device(): lax.psum_scatter(partial_value, 'layer', scatter_dimension=0, tiled=True)]
  transfers between devices with their start and end apart: 3 -> 9, of which waited for: 3 -> 8; matrix products, arithmetic and copies ran while one was open for 2% -> 8% of each run, Pallas kernels for 0% -> 0%
where the time goes in v1:
time: 152 us
  waiting for transfers between devices  94.3 us (62%)
  starting transfers between devices  16.3 us (11%)
  between operations  13.5 us (9%)
  local copies, waits for them, and re-layouts  12.5 us (8%)
  matrix products  10 us (7%)
  other arithmetic  4.85 us (3%)
    ppermute x7, waiting for transfers between devices, per_device(): lax.ppermute(ring[-1], 'row', [(dev, (dev + 1) % 8) for dev in range(8)])  48.1 us
    reduce_scatter x1, waiting for transfers between devices, per_device(): lax.psum_scatter(partial_value, 'layer', scatter_dimension=0, tiled=True)  46.2 us
    ppermute x7, starting transfers between devices, per_device(): lax.ppermute(ring[-1], 'row', [(dev, (dev + 1) % 8) for dev in range(8)])  16.3 us
    unnamed x20, local copies, waits for them, and re-layouts  11.2 us
    dot_general x1, matrix products, per_device(): jnp.dot(lax.all_gather(masked, 'col', axis=1, tiled=True), gathered, pref...  10 us
  transfers between devices with their start and end apart: 9, of which 8 were waited for; matrix products, arithmetic and copies ran while one was open for 8% of the time, Pallas kernels for 0%

profile of v1, /device:TPU:1, one launch (start us, length us, event | category | flops | bytes accessed | tf_op | source)
XLA Modules:
  0.0 151.6 jit_solution(17632208486148907574)
XLA Ops:
  7.3 2.2 %broadcast_multiply_fusion = bf16[2048,128]{1,0:T(8,128)(2,1)} fusion(bf16[2048,128]{1,0:T(8,128)(2,1)} %param.4, bf16[2048]{0:T(1024)(128)(2,1)S(1)} %broadcast_bitcast_fusion), kind=kLoop, calls=%fused_computation.4 | loop fusion | flops 262144 | bytes 1052672 | tf_op jit(solution)/shard_map/mul | solution.py:18
  9.6 4.8 %collective-permute-start = (bf16[256,384]{1,0:T(8,128)(2,1)}, bf16[256,384]{1,0:T(8,128)(2,1)S(1)}, u32[]{:S(2)}, u32[]{:S(2)}) collective-permute-start(bf16[256,384]{1,0:T(8,128)(2,1)} %param.5), channel_id=1, source_target_pairs={{0,64},{64,128},{128,192},{192,256},{256,320},{320,384},{384,448},... | collective-permute-start | bytes 589832 | tf_op jit(solution)/shard_map/ppermute | solution.py:12
  14.4 11.5 %collective-permute-done = bf16[256,384]{1,0:T(8,128)(2,1)S(1)} collective-permute-done((bf16[256,384]{1,0:T(8,128)(2,1)}, bf16[256,384]{1,0:T(8,128)(2,1)S(1)}, u32[]{:S(2)}, u32[]{:S(2)}) %collective-permute-start) | collective-permute-done | bytes 196640 | tf_op jit(solution)/shard_map/ppermute | solution.py:12
  25.9 1.9 %collective-permute-start.1 = (bf16[256,384]{1,0:T(8,128)(2,1)S(1)}, bf16[256,384]{1,0:T(8,128)(2,1)S(1)}, u32[]{:S(2)}, u32[]{:S(2)}) collective-permute-start(bf16[256,384]{1,0:T(8,128)(2,1)S(1)} %collective-permute-done), channel_id=1, source_target_pairs={{0,64},{64,128},{128,192},{192,256},{256,320},{320,384},{384,448},... | collective-permute-start | bytes 589832 | tf_op jit(solution)/shard_map/ppermute | solution.py:12
  27.8 6.4 %collective-permute-done.1 = bf16[256,384]{1,0:T(8,128)(2,1)S(1)} collective-permute-done((bf16[256,384]{1,0:T(8,128)(2,1)S(1)}, bf16[256,384]{1,0:T(8,128)(2,1)S(1)}, u32[]{:S(2)}, u32[]{:S(2)}) %collective-permute-start.1) | collective-permute-done | bytes 196640 | tf_op jit(solution)/shard_map/ppermute | solution.py:12
  34.3 1.9 %collective-permute-start.2 = (bf16[256,384]{1,0:T(8,128)(2,1)S(1)}, bf16[256,384]{1,0:T(8,128)(2,1)S(1)}, u32[]{:S(2)}, u32[]{:S(2)}) collective-permute-start(bf16[256,384]{1,0:T(8,128)(2,1)S(1)} %collective-permute-done.1), channel_id=1, source_target_pairs={{0,64},{64,128},{128,192},{192,256},{256,320},{320,384},{384,448},... | collective-permute-start | bytes 589832 | tf_op jit(solution)/shard_map/ppermute | solution.py:12
  36.2 6.1 %collective-permute-done.2 = bf16[256,384]{1,0:T(8,128)(2,1)S(1)} collective-permute-done((bf16[256,384]{1,0:T(8,128)(2,1)S(1)}, bf16[256,384]{1,0:T(8,128)(2,1)S(1)}, u32[]{:S(2)}, u32[]{:S(2)}) %collective-permute-start.2) | collective-permute-done | bytes 196640 | tf_op jit(solution)/shard_map/ppermute | solution.py:12
  42.3 1.9 %collective-permute-start.3 = (bf16[256,384]{1,0:T(8,128)(2,1)S(1)}, bf16[256,384]{1,0:T(8,128)(2,1)S(1)}, u32[]{:S(2)}, u32[]{:S(2)}) collective-permute-start(bf16[256,384]{1,0:T(8,128)(2,1)S(1)} %collective-permute-done.2), channel_id=1, source_target_pairs={{0,64},{64,128},{128,192},{192,256},{256,320},{320,384},{384,448},... | collective-permute-start | bytes 589832 | tf_op jit(solution)/shard_map/ppermute | solution.py:12
  44.2 6.1 %collective-permute-done.3 = bf16[256,384]{1,0:T(8,128)(2,1)S(1)} collective-permute-done((bf16[256,384]{1,0:T(8,128)(2,1)S(1)}, bf16[256,384]{1,0:T(8,128)(2,1)S(1)}, u32[]{:S(2)}, u32[]{:S(2)}) %collective-permute-start.3) | collective-permute-done | bytes 196640 | tf_op jit(solution)/shard_map/ppermute | solution.py:12
  50.3 1.9 %collective-permute-start.4 = (bf16[256,384]{1,0:T(8,128)(2,1)S(1)}, bf16[256,384]{1,0:T(8,128)(2,1)S(1)}, u32[]{:S(2)}, u32[]{:S(2)}) collective-permute-start(bf16[256,384]{1,0:T(8,128)(2,1)S(1)} %collective-permute-done.3), channel_id=1, source_target_pairs={{0,64},{64,128},{128,192},{192,256},{256,320},{320,384},{384,448},... | collective-permute-start | bytes 589832 | tf_op jit(solution)/shard_map/ppermute | solution.py:12
  52.2 6.1 %collective-permute-done.4 = bf16[256,384]{1,0:T(8,128)(2,1)S(1)} collective-permute-done((bf16[256,384]{1,0:T(8,128)(2,1)S(1)}, bf16[256,384]{1,0:T(8,128)(2,1)S(1)}, u32[]{:S(2)}, u32[]{:S(2)}) %collective-permute-start.4) | collective-permute-done | bytes 196640 | tf_op jit(solution)/shard_map/ppermute | solution.py:12
  58.3 1.9 %collective-permute-start.5 = (bf16[256,384]{1,0:T(8,128)(2,1)S(1)}, bf16[256,384]{1,0:T(8,128)(2,1)S(1)}, u32[]{:S(2)}, u32[]{:S(2)}) collective-permute-start(bf16[256,384]{1,0:T(8,128)(2,1)S(1)} %collective-permute-done.4), channel_id=1, source_target_pairs={{0,64},{64,128},{128,192},{192,256},{256,320},{320,384},{384,448},... | collective-permute-start | bytes 589832 | tf_op jit(solution)/shard_map/ppermute | solution.py:12
  60.2 6.1 %collective-permute-done.5 = bf16[256,384]{1,0:T(8,128)(2,1)S(1)} collective-permute-done((bf16[256,384]{1,0:T(8,128)(2,1)S(1)}, bf16[256,384]{1,0:T(8,128)(2,1)S(1)}, u32[]{:S(2)}, u32[]{:S(2)}) %collective-permute-start.5) | collective-permute-done | bytes 196640 | tf_op jit(solution)/shard_map/ppermute | solution.py:12
  66.3 1.9 %collective-permute-start.6 = (bf16[256,384]{1,0:T(8,128)(2,1)S(1)}, bf16[256,384]{1,0:T(8,128)(2,1)S(1)}, u32[]{:S(2)}, u32[]{:S(2)}) collective-permute-start(bf16[256,384]{1,0:T(8,128)(2,1)S(1)} %collective-permute-done.5), channel_id=1, source_target_pairs={{0,64},{64,128},{128,192},{192,256},{256,320},{320,384},{384,448},... | collective-permute-start | bytes 589832 | tf_op jit(solution)/shard_map/ppermute | solution.py:12
  68.3 5.8 %collective-permute-done.6 = bf16[256,384]{1,0:T(8,128)(2,1)S(1)} collective-permute-done((bf16[256,384]{1,0:T(8,128)(2,1)S(1)}, bf16[256,384]{1,0:T(8,128)(2,1)S(1)}, u32[]{:S(2)}, u32[]{:S(2)}) %collective-permute-start.6) | collective-permute-done | bytes 196640 | tf_op jit(solution)/shard_map/ppermute | solution.py:12
  76.9 0.7 constant_dynamic-update-slice_fusion.11
  78.3 0.7 constant_dynamic-update-slice_fusion.9
  80.4 0.7 constant_dynamic-update-slice_fusion.6
  82.5 0.7 constant_dynamic-update-slice_fusion.3
  83.9 0.7 constant_dynamic-update-slice_fusion.1
  84.6 0.7 constant_dynamic-update-slice_fusion
  85.3 10.0 %fusion = f32[2048,384]{1,0:T(8,128)} fusion(bf16[2048,2048]{1,0:T(8,128)(2,1)} %all-gather.2.cloned.1.call-done, bf16[4096,384]{1,0:T(8,128)(2,1)} %constant_dynamic-update-slice_fusion, s32[]{:T(128)S(6)} %select_n.14), kind=kOutput, calls=%fused_computation | convolution fusion | flops 3221225472 | bytes 13107204 | tf_op jit(solution)/shard_map/dot_general | solution.py:21
  96.6 46.2 %reduce-scatter.2.cloned.1.call-done = f32[512,384]{1,0:T(8,128)} async-done(((f32[2048,384]{1,0:T(8,128)}), f32[512,384]{1,0:T(8,128)}) %reduce-scatter.2.cloned.1.call-update) | async-done | bytes 786448 | tf_op jit(solution)/shard_map/reduce_scatter | solution.py:26
  142.8 2.0 %multiply_convert_fusion = bf16[512,384]{1,0:T(8,128)(2,1)} fusion(f32[512,384]{1,0:T(8,128)} %reduce-scatter.2.cloned.1.call-done, f32[512,384]{1,0:T(8,128)S(1)} %copy.6), kind=kLoop, calls=%fused_computation.3 | loop fusion | flops 393216 | bytes 1966080 | tf_op jit(solution)/shard_map/convert_element_type | solution.py:31
  (26 shorter events, 9.1 us)
Async XLA Ops:
  6.5 72.4 %copy-start = (bf16[256,384]{1,0:T(8,128)(2,1)S(1)}, bf16[256,384]{1,0:T(8,128)(2,1)}, u32[]{:S(2)}) copy-start(bf16[256,384]{1,0:T(8,128)(2,1)} %param.5) | copy-start | bytes 589828
  6.5 78.8 %all-gather.2.cloned.1.call-start = ((), (), s32[]{:S(2)}) async-start(), calls=%async_computation.1 | async-start | bytes 8912896 | tf_op jit(solution)/shard_map/all_gather | solution.py:22
  9.5 133.3 %reduce-scatter.2.cloned.1.call-start = ((), (), s32[]{:S(2)}) async-start(), calls=%async_computation.2 | async-start | bytes 3932160 | tf_op jit(solution)/shard_map/reduce_scatter | solution.py:26
  9.6 16.3 %collective-permute-start = (bf16[256,384]{1,0:T(8,128)(2,1)}, bf16[256,384]{1,0:T(8,128)(2,1)S(1)}, u32[]{:S(2)}, u32[]{:S(2)}) collective-permute-start(bf16[256,384]{1,0:T(8,128)(2,1)} %param.5), channel_id=1, source_target_pairs={{0,64},{64,128},{128,192},{192,256},{256,320},{320,384},{384,448},... | collective-permute-start | bytes 589832 | tf_op jit(solution)/shard_map/ppermute | solution.py:12
  25.9 8.4 %collective-permute-start.1 = (bf16[256,384]{1,0:T(8,128)(2,1)S(1)}, bf16[256,384]{1,0:T(8,128)(2,1)S(1)}, u32[]{:S(2)}, u32[]{:S(2)}) collective-permute-start(bf16[256,384]{1,0:T(8,128)(2,1)S(1)} %collective-permute-done), channel_id=1, source_target_pairs={{0,64},{64,128},{128,192},{192,256},{256,320},{320,384},{384,448},... | collective-permute-start | bytes 589832 | tf_op jit(solution)/shard_map/ppermute | solution.py:12
  34.3 8.0 %collective-permute-start.2 = (bf16[256,384]{1,0:T(8,128)(2,1)S(1)}, bf16[256,384]{1,0:T(8,128)(2,1)S(1)}, u32[]{:S(2)}, u32[]{:S(2)}) collective-permute-start(bf16[256,384]{1,0:T(8,128)(2,1)S(1)} %collective-permute-done.1), channel_id=1, source_target_pairs={{0,64},{64,128},{128,192},{192,256},{256,320},{320,384},{384,448},... | collective-permute-start | bytes 589832 | tf_op jit(solution)/shard_map/ppermute | solution.py:12
  42.3 8.0 %collective-permute-start.3 = (bf16[256,384]{1,0:T(8,128)(2,1)S(1)}, bf16[256,384]{1,0:T(8,128)(2,1)S(1)}, u32[]{:S(2)}, u32[]{:S(2)}) collective-permute-start(bf16[256,384]{1,0:T(8,128)(2,1)S(1)} %collective-permute-done.2), channel_id=1, source_target_pairs={{0,64},{64,128},{128,192},{192,256},{256,320},{320,384},{384,448},... | collective-permute-start | bytes 589832 | tf_op jit(solution)/shard_map/ppermute | solution.py:12
  50.3 8.0 %collective-permute-start.4 = (bf16[256,384]{1,0:T(8,128)(2,1)S(1)}, bf16[256,384]{1,0:T(8,128)(2,1)S(1)}, u32[]{:S(2)}, u32[]{:S(2)}) collective-permute-start(bf16[256,384]{1,0:T(8,128)(2,1)S(1)} %collective-permute-done.3), channel_id=1, source_target_pairs={{0,64},{64,128},{128,192},{192,256},{256,320},{320,384},{384,448},... | collective-permute-start | bytes 589832 | tf_op jit(solution)/shard_map/ppermute | solution.py:12
  58.3 8.0 %collective-permute-start.5 = (bf16[256,384]{1,0:T(8,128)(2,1)S(1)}, bf16[256,384]{1,0:T(8,128)(2,1)S(1)}, u32[]{:S(2)}, u32[]{:S(2)}) collective-permute-start(bf16[256,384]{1,0:T(8,128)(2,1)S(1)} %collective-permute-done.4), channel_id=1, source_target_pairs={{0,64},{64,128},{128,192},{192,256},{256,320},{320,384},{384,448},... | collective-permute-start | bytes 589832 | tf_op jit(solution)/shard_map/ppermute | solution.py:12
  66.3 7.7 %collective-permute-start.6 = (bf16[256,384]{1,0:T(8,128)(2,1)S(1)}, bf16[256,384]{1,0:T(8,128)(2,1)S(1)}, u32[]{:S(2)}, u32[]{:S(2)}) collective-permute-start(bf16[256,384]{1,0:T(8,128)(2,1)S(1)} %collective-permute-done.5), channel_id=1, source_target_pairs={{0,64},{64,128},{128,192},{192,256},{256,320},{320,384},{384,448},... | collective-permute-start | bytes 589832 | tf_op jit(solution)/shard_map/ppermute | solution.py:12
  95.3 0.7 copy-start.1
Sparse Core Ops, SparseCore 0:
  9.7 73.9 all-gather.1
  95.5 47.2 reduce-scatter.1
